TPU v7x, 32 devices: a whole 2x2x4 slice. The times are simulated.
32 devices in a mesh: grp: 2 (over x), pos: 16 (over z, y, core).
Axes of the slice: x: 2, y: 2, z: 4, core: 2. Of those that a mesh axis runs over, the one named last changes fastest.
Arguments:
- inputs: bfloat16 [768, 16, 512], P('grp', 'pos'), parts along dimension 0, may hold values from -6 to 6
- cotangent: bfloat16 [768, 16, 512], P('grp', 'pos'), parts along dimension 0, may hold values from -6 to 6
- col_weights: bfloat16 [4, 512, 512], replicated, may hold values from -0.25 to 0.25
- row_weights: bfloat16 [4, 512, 512], replicated, may hold values from -0.25 to 0.25
- read_start: int32 [768], P('grp'), parts along dimension 0, may hold values from 0 to 14, as said below
- read_end: int32 [768], P('grp'), parts along dimension 0, may hold values from 2 to 16, as said below
- windows: int32 [8], replicated, may hold values from 2 to 7
Outputs:
- input_grad: bfloat16 [768, 16, 512], P('grp', 'pos'), parts along dimension 0
- col_weight_grads: float32 [8, 512, 512], P('grp', 'pos'), parts along dimension 0
- row_weight_grads: float32 [8, 512, 512], P('grp', 'pos'), parts along dimension 0
There are 2 independent parts, one for each index of `grp`. A program takes and returns all parts, laid end to end along the dimension named above; an argument that names none is the same for every part. Nothing has to cross between parts.
Inputs may be any that keep to these rules, and one draw needn't show every extreme that they name: Read r covers positions read_start[r] to read_end[r] - 1, a span of 2 positions or more. read_end[r] - read_start[r] >= 2.
All inputs are finite; a program needn't handle non-finite values.
Results may differ from a plain program's by a relative error of at most 0.033.
The roundings to bfloat16 on the way count: a program that leaves them out, or rounds other values in their place, can miss the bound.
Values may be sent and summed in bfloat16 or wider, within the bound.
A program may use at most 128 MiB of HBM per device.

v0:
```python
import jax
import jax.numpy as jnp
from jax import lax
from jax.sharding import PartitionSpec as P

HEADS = 8


neg_fill = -1e30


def attend(scores, allowed, value_heads, form):
    masked = jnp.where(allowed, scores, neg_fill)
    highest = lax.stop_gradient(jnp.max(masked, axis=-1, keepdims=True))
    raised = jnp.exp(masked - highest)
    soft_weights = (raised / jnp.sum(raised, axis=-1, keepdims=True)).astype(jnp.bfloat16)
    return jnp.einsum(form, soft_weights.astype(jnp.float32), value_heads)


def col_core(queries, key_rows, value_rows, coverage):
    reads, local_pos, width = queries.shape
    heads_shape = (reads, local_pos, HEADS, width // HEADS)
    query_heads = queries.reshape(heads_shape).astype(jnp.float32)
    key_heads = key_rows.reshape(heads_shape).astype(jnp.float32)
    value_heads = value_rows.reshape(heads_shape).astype(jnp.float32)
    scores = jnp.einsum("iphe,jphe->phij", query_heads, key_heads) * (width // HEADS) ** (-0.5)
    allowed = (coverage.T[:, None, None, :] > 0.5) | jnp.eye(reads, dtype=bool)[None, None]
    mixed = attend(scores, allowed, value_heads, "phij,jphe->iphe")
    return mixed.reshape(queries.shape).astype(jnp.bfloat16)


def row_core(queries, key_rows, value_rows, coverage, windows):
    reads, length, width = queries.shape
    heads_shape = (reads, length, HEADS, width // HEADS)
    query_heads = queries.reshape(heads_shape).astype(jnp.float32)
    key_heads = key_rows.reshape(heads_shape).astype(jnp.float32)
    value_heads = value_rows.reshape(heads_shape).astype(jnp.float32)
    scores = jnp.einsum("bihe,bjhe->bhij", query_heads, key_heads) * (width // HEADS) ** (-0.5)
    places = jnp.arange(length)
    distance = jnp.abs(places[:, None] - places[None, :])
    in_window = distance[None] <= windows[:, None, None]
    covered = (coverage[:, None, None, :] > 0.5) | jnp.eye(length, dtype=bool)[None, None]
    allowed = in_window[None] & covered
    mixed = attend(scores, allowed, value_heads, "bhij,bjhe->bihe")
    return mixed.reshape(queries.shape).astype(jnp.bfloat16)


def projections(inputs, weights):
    width = inputs.shape[-1]
    flat_rows = inputs.reshape(-1, width)
    return tuple(
        (
            jnp.dot(flat_rows, weights[which], preferred_element_type=jnp.float32)
            .astype(jnp.bfloat16)
            .reshape(inputs.shape)
            for which in range(3)
        )
    )


def branch_forward(inputs, weights, coverage, core_apply):
    width = inputs.shape[-1]
    queries, key_rows, value_rows = projections(inputs, weights)
    mixed = core_apply(queries, key_rows, value_rows)
    output_proj = jnp.dot(
        mixed.reshape(-1, width), weights[3], preferred_element_type=jnp.float32
    ).reshape(inputs.shape)
    return (inputs.astype(jnp.float32) + output_proj * coverage[..., None]).astype(jnp.bfloat16)


def outer_sum(left, right):
    width = left.shape[-1]
    return jnp.dot(
        left.reshape(-1, width).T, right.reshape(-1, width), preferred_element_type=jnp.float32
    )


def branch_backward(inputs, upstream, weights, coverage, core_fn):
    width = inputs.shape[-1]
    queries, key_rows, value_rows = projections(inputs, weights)
    out_grad = (upstream.astype(jnp.float32) * coverage[..., None]).astype(jnp.bfloat16)
    mixed_grad = (
        jnp.dot(out_grad.reshape(-1, width), weights[3].T, preferred_element_type=jnp.float32)
        .astype(jnp.bfloat16)
        .reshape(inputs.shape)
    )
    mixed, pull = jax.vjp(core_fn, queries, key_rows, value_rows)
    query_grad, key_grad, value_grad = pull(mixed_grad)
    weight_terms = jnp.stack(
        [
            outer_sum(inputs, query_grad),
            outer_sum(inputs, key_grad),
            outer_sum(inputs, value_grad),
            outer_sum(mixed, out_grad),
        ]
    )
    back = upstream.astype(jnp.float32).reshape(-1, width)
    for which, grad_part in enumerate((query_grad, key_grad, value_grad)):
        back = back + jnp.dot(
            grad_part.reshape(-1, width), weights[which].T, preferred_element_type=jnp.float32
        )
    return (back.reshape(inputs.shape).astype(jnp.bfloat16), weight_terms)


def shards(inputs, cotangent, col_weights, row_weights, read_start, read_end, windows):
    reads, local_pos, width = inputs.shape
    ranks = lax.axis_size("pos")
    device = lax.axis_index("pos")
    local_ids = device * local_pos + jnp.arange(local_pos, dtype=jnp.int32)
    local_cover = (
        (local_ids[None, :] >= read_start[:, None]) & (local_ids[None, :] < read_end[:, None])
    ).astype(jnp.float32)

    def col_apply(queries, key_rows, value_rows):
        return col_core(queries, key_rows, value_rows, local_cover)

    hidden = branch_forward(inputs, col_weights, local_cover, col_apply)
    by_reads, grad_reads = (
        lax.all_to_all(hidden, "pos", split_axis=0, concat_axis=1, tiled=True),
        lax.all_to_all(cotangent, "pos", split_axis=0, concat_axis=1, tiled=True),
    )
    read_block = reads // ranks
    first_read = device * read_block
    span_first = lax.dynamic_slice_in_dim(read_start, first_read, read_block)
    span_last = lax.dynamic_slice_in_dim(read_end, first_read, read_block)
    every_pos = jnp.arange(local_pos * ranks, dtype=jnp.int32)
    read_cover = (
        (every_pos[None, :] >= span_first[:, None]) & (every_pos[None, :] < span_last[:, None])
    ).astype(jnp.float32)

    def row_apply(queries, key_rows, value_rows):
        return row_core(queries, key_rows, value_rows, read_cover, windows)

    hidden_grad, row_terms = branch_backward(
        by_reads, grad_reads, row_weights, read_cover, row_apply
    )
    position_grad = lax.all_to_all(hidden_grad, "pos", split_axis=1, concat_axis=0, tiled=True)
    input_grad, col_terms = branch_backward(
        inputs, position_grad, col_weights, local_cover, col_apply
    )
    col_sums, row_sums = (
        lax.psum_scatter(col_terms, "pos", scatter_dimension=1, tiled=True),
        lax.psum_scatter(row_terms, "pos", scatter_dimension=1, tiled=True),
    )
    return (input_grad, col_sums, row_sums)


def solution(mesh):
    return jax.shard_map(
        shards,
        mesh=mesh,
        in_specs=(P("grp", "pos", None), P("grp", "pos", None), P(), P(), P("grp"), P("grp"), P()),
        out_specs=(P("grp", "pos", None), P("grp", "pos", None), P("grp", "pos", None)),
        check_vma=False,
    )
```

profile of v0, /device:TPU:0, one launch (start us, length us, event | category | flops | bytes accessed | tf_op | source)
XLA Modules:
  0.0 341.8 jit_solution(13261961274836826562)
XLA Ops:
  12.6 3.8 %fusion.90 = (f32[8,384]{1,0:T(8,128)S(1)}, f32[8,384,384]{1,2,0:T(8,128)}) fusion(pred[384,384]{0,1:T(8,128)(4,1)S(1)} %fusion.39, bf16[384,8,64]{0,2,1:T(8,128)(2,1)S(1)} %bitcast.228, bf16[384,8,64]{0,2,1:T(8,128)(2,1)S(1)} %bitcast.226), kind=kOutput, calls=%fused_computation.145 | convolution fusion | flops 155713920 | bytes 5664768 | tf_op jit(solution)/shard_map/sub | solution.py:15
  16.4 2.7 divide_convert_fusion
  24.3 7.4 %all-to-all-start.1 = ((bf16[16,2,6144]{2,1,0:T(2,128)(2,1)}), bf16[16,2,6144]{2,1,0:T(2,128)(2,1)S(1)}, u32[]{:S(2)}, u32[]{:S(2)}) async-start(bf16[16,2,6144]{2,1,0:T(2,128)(2,1)} %reshape.437), calls=%async_computation.1 | async-start | bytes 786432 | tf_op jit(solution)/shard_map/all_to_all | solution.py:119
  35.9 8.0 %all-to-all-done.1 = bf16[16,2,6144]{2,1,0:T(2,128)(2,1)S(1)} async-done(((bf16[16,2,6144]{2,1,0:T(2,128)(2,1)}), bf16[16,2,6144]{2,1,0:T(2,128)(2,1)S(1)}, u32[]{:S(2)}, u32[]{:S(2)}) %all-to-all-start.1) | async-done | bytes 393248 | tf_op jit(solution)/shard_map/all_to_all | solution.py:119
  43.9 4.4 %all-to-all-start = ((bf16[16,2,6144]{2,1,0:T(2,128)(2,1)}), bf16[16,2,6144]{2,1,0:T(2,128)(2,1)}, u32[]{:S(2)}, u32[]{:S(2)}) async-start(bf16[16,2,6144]{2,1,0:T(2,128)(2,1)} %reshape.435), calls=%async_computation | async-start | bytes 786432 | tf_op jit(solution)/shard_map/all_to_all | solution.py:120
  48.9 2.3 convolution_convert_fusion.9
  52.8 7.6 %all-to-all-done = bf16[16,2,6144]{2,1,0:T(2,128)(2,1)} async-done(((bf16[16,2,6144]{2,1,0:T(2,128)(2,1)}), bf16[16,2,6144]{2,1,0:T(2,128)(2,1)}, u32[]{:S(2)}, u32[]{:S(2)}) %all-to-all-start) | async-done | bytes 393248 | tf_op jit(solution)/shard_map/all_to_all | solution.py:120
  60.3 3.5 %reshape.436 = bf16[384,1,512]{2,1,0:T(2,128)(2,1)} reshape(bf16[16,2,6144]{2,1,0:T(2,128)(2,1)} %all-to-all-done) | data formatting | bytes 786432
  68.5 2.3 reshape.412
  70.7 2.3 reshape_reshape.8
  75.9 4.5 %fusion.91 = (f32[24,8,16]{2,1,0:T(8,128)}, f32[24,8,16,16]{2,3,1,0:T(8,128)}) fusion(pred[24,16,16]{1,2,0:T(8,128)(4,1)} %broadcast_or_fusion, pred[8,16,16]{1,2,0:T(8,128)(4,1)} %broadcast_compare_fusion, bf16[24,16,8,64]{3,2,1,0:T(8,128)(2,1)} %reshape_reshape.8, bf16[24,16,8,64]{3,2,1,0:T(8,128)(2,1)} %reshape_reshape.7), kind=kOutput, calls=%fused_computation.146 | convolution fusion | flops 6537231 | bytes 1003520 | tf_op jit(solution)/shard_map/jvp()/sub | solution.py:15
  81.4 2.5 fusion.16
  92.6 2.4 copy.140
  96.8 2.4 copy.142
  99.1 2.4 reshape.419
  105.4 4.4 %all-to-all-start.2 = ((bf16[24,16,512]{2,0,1:T(8,128)(2,1)}), bf16[24,16,512]{2,0,1:T(8,128)(2,1)}, u32[]{:S(2)}, u32[]{:S(2)}) async-start(bf16[24,16,512]{2,0,1:T(8,128)(2,1)} %copy.144), calls=%async_computation.2 | async-start | bytes 786432 | tf_op jit(solution)/shard_map/all_to_all | solution.py:137
  110.5 11.5 %all-to-all-done.2 = bf16[24,16,512]{2,0,1:T(8,128)(2,1)} async-done(((bf16[24,16,512]{2,0,1:T(8,128)(2,1)}), bf16[24,16,512]{2,0,1:T(8,128)(2,1)}, u32[]{:S(2)}, u32[]{:S(2)}) %all-to-all-start.2) | async-done | bytes 393248 | tf_op jit(solution)/shard_map/all_to_all | solution.py:137
  125.3 2.6 convolution_bitcast_fusion.4
  132.0 3.4 fusion.7
  140.3 2.5 pad_maximum_fusion
  142.8 5.5 %copy.150 = f32[4,512,512]{2,0,1:T(4,128)} copy(f32[4,512,512]{1,2,0:T(8,128)} %pad_maximum_fusion) | data formatting | bytes 8388608 | tf_op jit(solution)/shard_map/stack | solution.py:89
  154.4 2.5 pad_maximum_fusion.1
  161.9 96.9 %all-reduce.3.cloned.1.call-done = f32[4,512,512]{2,0,1:T(4,128)} async-done(((f32[4,512,512]{2,0,1:T(4,128)}), f32[4,512,512]{2,0,1:T(4,128)}) %all-reduce.3.cloned.1.call-update) | async-done | bytes 4194320
  260.5 74.5 %reduce-scatter.2.cloned.1.call-done = f32[4,32,512]{2,1,0:T(8,128)} async-done(((f32[4,512,512]{2,1,0:T(8,128)}), f32[4,32,512]{2,1,0:T(8,128)}) %reduce-scatter.2.cloned.1.call-update) | async-done | bytes 262160 | tf_op jit(solution)/shard_map/reduce_scatter | solution.py:143
  (178 shorter events, 64.2 us)
Async XLA Ops:
  7.2 4.6 %copy-start.45 = (s32[384]{0:T(512)S(1)}, s32[384]{0:T(512)}, u32[]{:S(2)}) copy-start(s32[384]{0:T(512)} %param.11) | copy-start | bytes 4612
  7.2 4.6 %copy-start.46 = (s32[384]{0:T(512)S(1)}, s32[384]{0:T(512)}, u32[]{:S(2)}) copy-start(s32[384]{0:T(512)} %param.12) | copy-start | bytes 4612
  11.9 4.5 %copy-start.36 = (pred[384,384]{0,1:T(8,128)(4,1)}, pred[384,384]{0,1:T(8,128)(4,1)S(1)}, u32[]{:S(2)}) copy-start(pred[384,384]{0,1:T(8,128)(4,1)S(1)} %fusion.39) | copy-start | bytes 442372
  12.1 4.3 %copy-start.33 = (bf16[384,512]{0,1:T(8,128)(2,1)}, bf16[384,512]{0,1:T(8,128)(2,1)S(1)}, u32[]{:S(2)}) copy-start(bf16[384,512]{0,1:T(8,128)(2,1)S(1)} %copy.130) | copy-start | bytes 1179652
  12.4 4.1 %copy-start.31 = (bf16[384,512]{0,1:T(8,128)(2,1)}, bf16[384,512]{0,1:T(8,128)(2,1)S(1)}, u32[]{:S(2)}) copy-start(bf16[384,512]{0,1:T(8,128)(2,1)S(1)} %copy.131) | copy-start | bytes 1179652
  12.6 6.6 %copy-start.3 = (bf16[384,512]{0,1:T(8,128)(2,1)}, bf16[384,512]{0,1:T(8,128)(2,1)S(1)}, u32[]{:S(2)}) copy-start(bf16[384,512]{0,1:T(8,128)(2,1)S(1)} %copy.129) | copy-start | bytes 1179652
  20.5 11.5 %copy-start.35 = (bf16[384,1,512]{2,0,1:T(8,128)(2,1)S(1)}, bf16[384,1,512]{2,0,1:T(8,128)(2,1)}, u32[]{:S(2)}) copy-start(bf16[384,1,512]{2,0,1:T(8,128)(2,1)} %param.8) | copy-start | bytes 1179652
  24.3 19.6 %all-to-all-start.1 = ((bf16[16,2,6144]{2,1,0:T(2,128)(2,1)}), bf16[16,2,6144]{2,1,0:T(2,128)(2,1)S(1)}, u32[]{:S(2)}, u32[]{:S(2)}) async-start(bf16[16,2,6144]{2,1,0:T(2,128)(2,1)} %reshape.437), calls=%async_computation.1 | async-start | bytes 786432 | tf_op jit(solution)/shard_map/all_to_all | solution.py:119
  43.9 16.4 %all-to-all-start = ((bf16[16,2,6144]{2,1,0:T(2,128)(2,1)}), bf16[16,2,6144]{2,1,0:T(2,128)(2,1)}, u32[]{:S(2)}, u32[]{:S(2)}) async-start(bf16[16,2,6144]{2,1,0:T(2,128)(2,1)} %reshape.435), calls=%async_computation | async-start | bytes 786432 | tf_op jit(solution)/shard_map/all_to_all | solution.py:120
  65.0 3.5 %copy-start = (bf16[384,1,512]{2,0,1:T(8,128)(2,1)}, bf16[384,1,512]{2,0,1:T(8,128)(2,1)S(1)}, u32[]{:S(2)}) copy-start(bf16[384,1,512]{2,0,1:T(8,128)(2,1)S(1)} %copy.124) | copy-start | bytes 1179652
  75.9 5.5 %copy-start.17 = (bf16[24,16,8,64]{3,2,1,0:T(8,128)(2,1)}, bf16[24,16,8,64]{3,2,1,0:T(8,128)(2,1)S(1)}, u32[]{:S(2)}) copy-start(bf16[24,16,8,64]{3,2,1,0:T(8,128)(2,1)S(1)} %reshape_reshape.6) | copy-start | bytes 1179652
  92.6 11.4 %copy-start.12 = (bf16[384,512]{1,0:T(8,128)(2,1)}, bf16[384,512]{1,0:T(8,128)(2,1)S(1)}, u32[]{:S(2)}) copy-start(bf16[384,512]{1,0:T(8,128)(2,1)S(1)} %reshape.420) | copy-start | bytes 1179652
  96.7 6.6 %copy-start.10 = (bf16[384,512]{1,0:T(8,128)(2,1)}, bf16[384,512]{1,0:T(8,128)(2,1)S(1)}, u32[]{:S(2)}) copy-start(bf16[384,512]{1,0:T(8,128)(2,1)S(1)} %reshape.418) | copy-start | bytes 1179652
  104.0 5.9 %copy-start.42 = (f32[8,384]{1,0:T(8,128)S(1)}, f32[8,384]{1,0:T(8,128)}, u32[]{:S(2)}) copy-start(f32[8,384]{1,0:T(8,128)} %copy-done.41) | copy-start | bytes 36868
  105.4 16.7 %all-to-all-start.2 = ((bf16[24,16,512]{2,0,1:T(8,128)(2,1)}), bf16[24,16,512]{2,0,1:T(8,128)(2,1)}, u32[]{:S(2)}, u32[]{:S(2)}) async-start(bf16[24,16,512]{2,0,1:T(8,128)(2,1)} %copy.144), calls=%async_computation.2 | async-start | bytes 786432 | tf_op jit(solution)/shard_map/all_to_all | solution.py:137
  109.8 148.9 %all-reduce.3.cloned.1.call-start = ((), (), s32[]{:S(2)}) async-start(), calls=%async_computation.5 | async-start | bytes 8388608
  129.9 5.6 %slice-start = ((s8[4718592]{0:T(1024)(128)(4,1)}), s8[4194304]{0:T(1024)(128)(4,1)S(1)}, s32[]{:S(2)}) async-start(s8[4718592]{0:T(1024)(128)(4,1)} %bitcast.197), calls=%async_computation.6 | async-start | bytes 8388608
  132.0 6.7 %copy-start.8 = (bf16[8,64,384]{2,1,0:T(8,128)(2,1)}, bf16[8,64,384]{2,1,0:T(8,128)(2,1)S(1)}, u32[]{:S(2)}) copy-start(bf16[8,64,384]{2,1,0:T(8,128)(2,1)S(1)} %convolution_convert_fusion.16) | copy-start | bytes 1179652
  132.0 3.5 %slice-start.1 = ((s8[4718592]{0:T(1024)(128)(4,1)}), s8[524288]{0:T(1024)(128)(4,1)S(1)}, s32[]{:S(2)}) async-start(s8[4718592]{0:T(1024)(128)(4,1)} %bitcast.197), calls=%async_computation.7 | async-start | bytes 1048576
  132.0 3.5 %copy-start.34 = (bf16[384,512]{0,1:T(8,128)(2,1)S(1)}, bf16[384,512]{0,1:T(8,128)(2,1)}, u32[]{:S(2)}) copy-start(bf16[384,512]{0,1:T(8,128)(2,1)} %copy-done.33) | copy-start | bytes 1179652
  132.0 3.5 %copy-start.37 = (pred[384,384]{0,1:T(8,128)(4,1)S(1)}, pred[384,384]{0,1:T(8,128)(4,1)}, u32[]{:S(2)}) copy-start(pred[384,384]{0,1:T(8,128)(4,1)} %copy-done.36) | copy-start | bytes 442372
  132.0 3.5 %copy-start.43 = (f32[8,384]{1,0:T(8,128)S(1)}, f32[8,384]{1,0:T(8,128)}, u32[]{:S(2)}) copy-start(f32[8,384]{1,0:T(8,128)} %copy-done.41) | copy-start | bytes 36868
  148.3 186.7 %reduce-scatter.2.cloned.1.call-start = ((), (), s32[]{:S(2)}) async-start(), calls=%async_computation.4 | async-start | bytes 4456448 | tf_op jit(solution)/shard_map/reduce_scatter | solution.py:143
  156.9 3.4 copy-start.23
  (31 other events, 56.2 us)
Sparse Core Ops, SparseCore 0:
  148.4 110.3 all-reduce.2
  263.7 71.2 reduce-scatter.1
where the time goes:
time: 343 us; the launch traced here: 342 us
  waiting for transfers between devices  198 us (58%)
  matrix products  50.7 us (15%)
  local copies, waits for them, and re-layouts  45 us (13%)
  starting transfers between devices  16.3 us (5%)
  other arithmetic  15.7 us (5%)
  between operations  15.6 us (5%)
    unnamed x3, waiting for transfers between devices  96.9 us
    reduce_scatter x1, waiting for transfers between devices, shards(): lax.psum_scatter(row_terms, 'pos', scatter_dimension=1, tiled=True)  74.5 us
    unnamed x109, local copies, waits for them, and re-layouts  13.3 us
    all_to_all x1, waiting for transfers between devices, shards(): lax.all_to_all(hidden_grad, 'pos', split_axis=1, concat_axis=0, tiled=True)  11.5 us
    dot_general x6, matrix products, attend(): return jnp.einsum(form, soft_weights.astype(jnp.float32), value_heads)  10.3 us
    sub x2, matrix products, attend(): raised = jnp.exp(masked - highest)  8.36 us
    dot_general x6, matrix products, projections(): jnp.dot(flat_rows, weights[which], preferred_element_type=jnp.float32)  8.34 us
    all_to_all x1, waiting for transfers between devices, shards(): lax.all_to_all(hidden, 'pos', split_axis=0, concat_axis=1, tiled=True)  8.02 us
  transfers between devices with their start and end apart: 5, of which 5 were waited for; matrix products, arithmetic and copies ran while one was open for 6% of the time, Pallas kernels for 0%

commit v1 on v0

v1 whole, which is shorter than its diff:
```python
import functools

import jax
import jax.numpy as jnp
from jax import lax
from jax.experimental import pallas as pl
from jax.experimental.pallas import tpu as pltpu
from jax.sharding import PartitionSpec as P

HEADS = 8
LANES = 128
NEG = -1e30
FAR = 1e9
VMEM_LIMIT = 56 * 1024 * 1024
f32, bf16 = jnp.float32, jnp.bfloat16


def dot_nn(a, b):
    return lax.dot_general(a, b, (((1,), (0,)), ((), ())), preferred_element_type=f32)


def dot_nt(a, b):
    return lax.dot_general(a, b, (((1,), (1,)), ((), ())), preferred_element_type=f32)


def dot_tn(a, b):
    return lax.dot_general(a, b, (((0,), (0,)), ((), ())), preferred_element_type=f32)


def project(x_ref, w_ref, q_ref, k_ref, v_ref):
    x = x_ref[...]
    q_ref[...] = (dot_nn(x, w_ref[0]) * 0.125).astype(bf16)
    k_ref[...] = dot_nn(x, w_ref[1]).astype(bf16)
    v_ref[...] = dot_nn(x, w_ref[2]).astype(bf16)


def probs_t(k2, qm, dist, width):
    s = jnp.where(dist <= width, dot_nt(k2, qm), NEG)
    e = jnp.exp(s - jnp.max(s, axis=0, keepdims=True))
    return e * (1.0 / jnp.sum(e, axis=0, keepdims=True))


def halves(pair):
    lane = lax.broadcasted_iota(jnp.int32, pair.shape, 1)
    low = lane < LANES // 2
    zero = jnp.zeros_like(pair)
    return jnp.where(low, pair, zero), jnp.where(low, zero, pair)


def merge(a, b):
    lane = lax.broadcasted_iota(jnp.int32, a.shape, 1)
    return jnp.where(lane < LANES // 2, a, b)


def forward_pairs(q_ref, k_ref, v_ref, dist_ref, m_ref):
    @pl.loop(0, HEADS // 2)
    def _(pair):
        at = pl.ds(pl.multiple_of(pair * LANES, LANES), LANES)
        k2, v2 = k_ref[:, at], v_ref[:, at]
        outs = []
        for qm in halves(q_ref[:, at]):
            p = probs_t(k2, qm, dist_ref[...], 0.5).astype(bf16)
            outs.append(dot_tn(p, v2))
        m_ref[:, at] = merge(*outs).astype(bf16)


def backward_pairs(q_ref, k_ref, v_ref, g_ref, dist_ref, width_of, m_ref, dq_ref, dk_ref, dv_ref):
    @pl.loop(0, HEADS // 2)
    def _(pair):
        at = pl.ds(pl.multiple_of(pair * LANES, LANES), LANES)
        k2, v2 = k_ref[:, at], v_ref[:, at]
        q_parts, g_parts = halves(q_ref[:, at]), halves(g_ref[:, at])
        outs, dqs, dk, dv = [], [], 0.0, 0.0
        for which in range(2):
            qm, gm = q_parts[which], g_parts[which]
            p = probs_t(k2, qm, dist_ref[...], width_of(pair * 2 + which))
            pb = p.astype(bf16)
            if m_ref is not None:
                outs.append(dot_tn(pb, v2))
            dp = dot_nt(v2, gm).astype(bf16).astype(f32)
            ds = (p * (dp - jnp.sum(dp * p, axis=0, keepdims=True))).astype(bf16)
            dv = dv + dot_nn(pb, gm)
            dk = dk + dot_nn(ds, qm)
            dqs.append(dot_tn(ds, k2))
        if m_ref is not None:
            m_ref[:, at] = merge(*outs).astype(bf16)
        dq_ref[:, at] = (merge(*dqs) * 0.125).astype(bf16)
        dk_ref[:, at] = dk.astype(bf16)
        dv_ref[:, at] = dv.astype(bf16)


def col_dist(dist_ref, cov):
    n = dist_ref.shape[0]
    j = lax.broadcasted_iota(jnp.int32, (n, n), 0)
    i = lax.broadcasted_iota(jnp.int32, (n, n), 1)
    dist_ref[...] = jnp.where((cov > 0.5) | (i == j), 0.0, FAR)


def finish(x_ref, up_ref, cov, w_ref, m_ref, og_ref, dq_ref, dk_ref, dv_ref, back_ref, terms_ref):
    x = x_ref[...]
    for which, grad_ref in enumerate((dq_ref, dk_ref, dv_ref)):
        terms_ref[which] = dot_tn(x, grad_ref[...]).astype(bf16)
    terms_ref[3] = dot_tn(m_ref[...], og_ref[...]).astype(bf16)


def back_sum(up_ref, w_ref, dq_ref, dk_ref, dv_ref, back_ref):
    back = up_ref[...].astype(f32)
    for which, grad_ref in enumerate((dq_ref, dk_ref, dv_ref)):
        back = back + dot_nt(grad_ref[...], w_ref[which])
    back_ref[...] = back.astype(bf16)


def col_forward(x_ref, w_ref, cov_ref, q_ref, k_ref, v_ref, m_ref, h_ref, dist_ref):
    cov = cov_ref[...]
    col_dist(dist_ref, cov)
    project(x_ref, w_ref, q_ref, k_ref, v_ref)
    forward_pairs(q_ref, k_ref, v_ref, dist_ref, m_ref)
    out = dot_nn(m_ref[...], w_ref[3])
    h_ref[...] = (x_ref[...].astype(f32) + out * cov).astype(bf16)


def row_both(
    h_ref, up_ref, w_ref, cov_ref, sub_ref, lane_ref, windows_ref, back_ref, terms_ref,
    q_ref, k_ref, v_ref, m_ref, og_ref, g_ref, dq_ref, dk_ref, dv_ref, dist_ref,
):
    cov = cov_ref[...]
    gap = jnp.abs(sub_ref[:, 0:1] - lane_ref[0:1, :])
    same = sub_ref[:, 1:2] == lane_ref[1:2, :]
    dist_ref[...] = jnp.where(same & ((cov > 0.5) | (gap == 0.0)), gap, FAR)
    project(h_ref, w_ref, q_ref, k_ref, v_ref)
    og_ref[...] = (up_ref[...].astype(f32) * cov).astype(bf16)
    g_ref[...] = dot_nt(og_ref[...], w_ref[3]).astype(bf16)
    backward_pairs(
        q_ref, k_ref, v_ref, g_ref, dist_ref,
        lambda head: windows_ref[head].astype(f32), m_ref, dq_ref, dk_ref, dv_ref,
    )
    back_sum(up_ref, w_ref, dq_ref, dk_ref, dv_ref, back_ref)
    finish(h_ref, up_ref, cov, w_ref, m_ref, og_ref, dq_ref, dk_ref, dv_ref, back_ref, terms_ref)


def col_backward(
    x_ref, up_ref, w_ref, cov_ref, q_ref, k_ref, v_ref, m_ref, back_ref, terms_ref,
    og_ref, g_ref, dq_ref, dk_ref, dv_ref, dist_ref,
):
    cov = cov_ref[...]
    col_dist(dist_ref, cov)
    og_ref[...] = (up_ref[...].astype(f32) * cov).astype(bf16)
    g_ref[...] = dot_nt(og_ref[...], w_ref[3]).astype(bf16)
    backward_pairs(
        q_ref, k_ref, v_ref, g_ref, dist_ref, lambda head: 0.5, None, dq_ref, dk_ref, dv_ref
    )
    back_sum(up_ref, w_ref, dq_ref, dk_ref, dv_ref, back_ref)
    finish(x_ref, up_ref, cov, w_ref, m_ref, og_ref, dq_ref, dk_ref, dv_ref, back_ref, terms_ref)


def reduce_rows(terms, ranks, me):
    width = terms.shape[-1]
    held = terms.reshape(4, ranks, width // ranks, width)
    bit = 0
    while (1 << bit) < ranks:
        mine = (me >> bit) & 1
        blocks = held.shape[1] // 2
        split = held.reshape(4, blocks, 2, width // ranks, width)
        keep = lax.dynamic_index_in_dim(split, mine, 2, keepdims=False)
        give = lax.dynamic_index_in_dim(split, 1 - mine, 2, keepdims=False)
        got = lax.ppermute(give, "pos", [(r, r ^ (1 << bit)) for r in range(ranks)])
        total = keep.astype(f32) + got.astype(f32)
        bit += 1
        held = total if (1 << bit) >= ranks else total.astype(bf16)
    return held[:, 0]


def shards(inputs, cotangent, col_weights, row_weights, read_start, read_end, windows):
    reads, local_pos, width = inputs.shape
    ranks = lax.axis_size("pos")
    me = lax.axis_index("pos")
    block = reads // ranks
    rows = reads
    x = inputs.reshape(rows, width)
    cov = ((me >= read_start) & (me < read_end)).astype(f32)[:, None]
    start_here = lax.dynamic_slice_in_dim(read_start, me * block, block)
    end_here = lax.dynamic_slice_in_dim(read_end, me * block, block)
    place = jnp.arange(ranks, dtype=jnp.int32)[:, None]
    row_cov = ((place >= start_here[None]) & (place < end_here[None])).astype(f32).reshape(rows, 1)
    ids = jnp.arange(rows, dtype=jnp.int32)
    lanes = jnp.stack([ids // block, ids % block]).astype(f32)
    subs = lanes.T

    act = jax.ShapeDtypeStruct((rows, width), bf16)
    terms = jax.ShapeDtypeStruct((4, width, width), bf16)
    vm = pltpu.VMEM((rows, width), bf16)
    dist = pltpu.VMEM((rows, rows), f32)
    params = pltpu.CompilerParams(vmem_limit_bytes=VMEM_LIMIT)
    swap = functools.partial(lax.all_to_all, axis_name="pos", split_axis=0, concat_axis=0, tiled=True)

    def spread(array):
        return swap(array.reshape(ranks, block, width)).reshape(rows, width)

    up_rows = spread(cotangent.reshape(rows, width))
    q, k, v, mixed, hidden = pl.pallas_call(
        col_forward, out_shape=[act] * 5, scratch_shapes=[dist], compiler_params=params
    )(x, col_weights, cov)
    hid_rows = spread(hidden)
    spec = pl.BlockSpec(memory_space=pltpu.VMEM)
    back, row_terms = pl.pallas_call(
        row_both,
        out_shape=[act, terms],
        in_specs=[spec] * 6 + [pl.BlockSpec(memory_space=pltpu.SMEM)],
        scratch_shapes=[vm] * 9 + [dist],
        compiler_params=params,
    )(hid_rows, up_rows, row_weights, row_cov, subs, lanes, windows)
    up_cols = spread(back)
    grad, col_terms = pl.pallas_call(
        col_backward,
        out_shape=[act, terms],
        scratch_shapes=[vm] * 5 + [dist],
        compiler_params=params,
    )(x, up_cols, col_weights, cov, q, k, v, mixed)
    row_sums = reduce_rows(row_terms, ranks, me)
    col_sums = reduce_rows(col_terms, ranks, me)
    return (grad.reshape(inputs.shape), col_sums, row_sums)


def solution(mesh):
    return jax.shard_map(
        shards,
        mesh=mesh,
        in_specs=(P("grp", "pos", None), P("grp", "pos", None), P(), P(), P("grp"), P("grp"), P()),
        out_specs=(P("grp", "pos", None), P("grp", "pos", None), P("grp", "pos", None)),
        check_vma=False,
    )
```

time: 343 us -> 139 us (0.41)
  waiting for transfers between devices: 198 us -> 52.3 us
  matrix products: 50.7 us -> 0 us
  Pallas kernels: 0 us -> 34.1 us
  local copies, waits for them, and re-layouts: 45 us -> 12.1 us
  blocking collectives: 0 us -> 19.7 us
  between operations: 15.6 us -> 0.75 us
  other arithmetic: 15.7 us -> 6.61 us
    unnamed x3 -> x0, waiting for transfers between devices: 96.9 us -> none
    reduce_scatter x1 -> x0, waiting for transfers between devices: 74.5 us -> none  [shards(): lax.psum_scatter(row_terms, 'pos', scatter_dimension=1, tiled=True)]
    dot_general x33 -> x0, matrix products: 42.4 us -> none  [the longest x6 10.3 us: attend(): return jnp.einsum(form, soft_weights.astype(jnp.float32), value_heads)]
    ppermute x0 -> x8, waiting for transfers between devices: none -> 34.5 us  [reduce_rows(): got = lax.ppermute(give, 'pos', [(r, r ^ 1 << bit) for r in range(ranks)])]
    pallas_call x0 -> x3, Pallas kernels: none -> 34.1 us  [the longest x1 14 us: shards(): pl.pallas_call(row_both, out_shape=[act, terms], in_specs=[spec] * 6 + [p...]
    all_to_all x0 -> x1, blocking collectives: none -> 19.7 us  [spread(): return swap(array.reshape(ranks, block, width)).reshape(rows, width)]
    unnamed x109 -> x8, local copies, waits for them, and re-layouts: 13.3 us -> 1.55 us
    convert_element_type x12 -> x1, local copies, waits for them, and re-layouts: 11.5 us -> 0.8 us  [shards(): ((place >= start_here[None]) & (place < end_here[None])).astype(f32)]
  transfers between devices with their start and end apart: 5 -> 10, of which waited for: 5 -> 6; matrix products, arithmetic and copies ran while one was open for 6% -> 11% of each run, Pallas kernels for 0% -> 9%
where the time goes in v1:
time: 139 us
  waiting for transfers between devices  52.3 us (38%)
  Pallas kernels  34.1 us (25%)
  blocking collectives  19.7 us (14%)
  starting transfers between devices  13.1 us (9%)
  local copies, waits for them, and re-layouts  12.1 us (9%)
  other arithmetic  6.61 us (5%)
    ppermute x8, waiting for transfers between devices, reduce_rows(): got = lax.ppermute(give, 'pos', [(r, r ^ 1 << bit) for r in range(ranks)])  34.5 us
    all_to_all x1, blocking collectives, spread(): return swap(array.reshape(ranks, block, width)).reshape(rows, width)  19.7 us
    all_to_all x2, waiting for transfers between devices, spread(): return swap(array.reshape(ranks, block, width)).reshape(rows, width)  17.9 us
    pallas_call x1, Pallas kernels, shards(): pl.pallas_call(row_both, out_shape=[act, terms], in_specs=[spec] * 6 + [p...  14 us
    pallas_call x1, Pallas kernels, shards(): pl.pallas_call(col_backward, out_shape=[act, terms], scratch_shapes=[vm]...  12.1 us
    pallas_call x1, Pallas kernels, shards(): pl.pallas_call(col_forward, out_shape=[act] * 5, scratch_shapes=[dist], c...  7.9 us
    all_to_all x2, starting transfers between devices, spread(): return swap(array.reshape(ranks, block, width)).reshape(rows, width)  7.29 us
    squeeze x8, local copies, waits for them, and re-layouts, reduce_rows(): give = lax.dynamic_index_in_dim(split, 1 - mine, 2, keepdims=False)  6.66 us
  transfers between devices with their start and end apart: 10, of which 6 were waited for; matrix products, arithmetic and copies ran while one was open for 11% of the time, Pallas kernels for 9%

profile of v1, /device:TPU:0, one launch (start us, length us, event | category | flops | bytes accessed | tf_op | source)
XLA Modules:
  0.0 138.7 jit_solution(15463604146780369907)
XLA Ops:
  2.1 7.9 %shard_map.94 = (bf16[384,512]{1,0:T(8,128)(2,1)}, bf16[384,512]{1,0:T(8,128)(2,1)}, bf16[384,512]{1,0:T(8,128)(2,1)}, bf16[384,512]{1,0:T(8,128)(2,1)}, bf16[384,512]{1,0:T(8,128)(2,1)}) custom-call(bf16[384,512]{1,0:T(8,128)(2,1)} %bitcast.67, bf16[4,512,512]{2,1,0:T(8,128)(2,1)} %w_ref.5, f32[384,1]{1,0:T(8,128)} %reshape.187.cov_ref), custom_call_target="tpu_custom_call" | custom-call | tf_op jit(solution)/shard_map/pallas_call | solution.py:200
  10.0 19.7 %all_to_all.15 = bf16[16,24,512]{2,1,0:T(8,128)(2,1)} all-to-all(bf16[16,24,512]{2,1,0:T(8,128)(2,1)} %bitcast.72), channel_id=1, replica_groups=mesh['grp'=2,'pos'=16] {'pos'}, dimensions={0} | all-to-all | bytes 786432 | tf_op jit(solution)/shard_map/all_to_all | solution.py:197
  29.7 3.6 %all-to-all-start.1 = ((bf16[16,24,512]{2,1,0:T(8,128)(2,1)}), bf16[16,24,512]{2,1,0:T(8,128)(2,1)S(1)}, u32[]{:S(2)}, u32[]{:S(2)}) async-start(bf16[16,24,512]{2,1,0:T(8,128)(2,1)} %bitcast.3), calls=%async_computation.1 | async-start | bytes 786432 | tf_op jit(solution)/shard_map/all_to_all | solution.py:197
  36.2 0.8 copy.17.sub_ref
  37.0 8.4 %all-to-all-done.1 = bf16[16,24,512]{2,1,0:T(8,128)(2,1)S(1)} async-done(((bf16[16,24,512]{2,1,0:T(8,128)(2,1)}), bf16[16,24,512]{2,1,0:T(8,128)(2,1)S(1)}, u32[]{:S(2)}, u32[]{:S(2)}) %all-to-all-start.1) | async-done | bytes 393248 | tf_op jit(solution)/shard_map/all_to_all | solution.py:197
  46.2 14.0 %shard_map.95 = (bf16[384,512]{1,0:T(8,128)(2,1)}, bf16[4,512,512]{2,1,0:T(8,128)(2,1)}) custom-call(bf16[384,512]{1,0:T(8,128)(2,1)} %bitcast.69, bf16[384,512]{1,0:T(8,128)(2,1)} %bitcast.70, bf16[4,512,512]{2,1,0:T(8,128)(2,1)} %w_ref.4, f32[384,1]{1,0:T(8,128)} %reshape.188.cov_ref, f32[384,2]{1,0:T(8,128)} %copy.17.sub_ref, ...), custom_call_target="tpu_custom_call" | custom-call | tf_op jit(solution)/shard_map/pallas_call | solution.py:205
  60.2 3.7 %all-to-all-start.2 = ((bf16[16,24,512]{2,1,0:T(8,128)(2,1)}), bf16[16,24,512]{2,1,0:T(8,128)(2,1)S(1)}, u32[]{:S(2)}, u32[]{:S(2)}) async-start(bf16[16,24,512]{2,1,0:T(8,128)(2,1)} %bitcast.71), calls=%async_computation.2 | async-start | bytes 786432 | tf_op jit(solution)/shard_map/all_to_all | solution.py:197
  64.0 2.4 %dynamic-slice_bitcast_fusion = bf16[4,8,32,512]{3,2,1,0:T(8,128)(2,1)} fusion(bf16[4,8,2,32,512]{4,3,2,1,0:T(8,128)(2,1)} %bitcast.58, s32[]{:T(128)S(6)} %select_n.70), kind=kLoop, calls=%fused_computation.8 | loop fusion | bytes 2097156 | tf_op jit(solution)/shard_map/jit(dynamic_index_in_dim)/squeeze | solution.py:165
  66.5 9.4 %all-to-all-done.2 = bf16[16,24,512]{2,1,0:T(8,128)(2,1)S(1)} async-done(((bf16[16,24,512]{2,1,0:T(8,128)(2,1)}), bf16[16,24,512]{2,1,0:T(8,128)(2,1)S(1)}, u32[]{:S(2)}, u32[]{:S(2)}) %all-to-all-start.2) | async-done | bytes 393248 | tf_op jit(solution)/shard_map/all_to_all | solution.py:197
  76.7 12.1 %shard_map.96 = (bf16[384,512]{1,0:T(8,128)(2,1)}, bf16[4,512,512]{2,1,0:T(8,128)(2,1)}) custom-call(bf16[384,512]{1,0:T(8,128)(2,1)} %bitcast.68, bf16[384,512]{1,0:T(8,128)(2,1)} %bitcast.66, bf16[4,512,512]{2,1,0:T(8,128)(2,1)} %w_ref.5, f32[384,1]{1,0:T(8,128)} %reshape.187.cov_ref, bf16[384,512]{1,0:T(8,128)(2,1)} %get-tuple-element.14.q_ref, ...), custom_call_target="tpu_custom_call" | custom-call | tf_op jit(solution)/shard_map/pallas_call | solution.py:213
  88.9 2.5 %dynamic-slice_bitcast_fusion.1 = bf16[4,8,32,512]{3,2,1,0:T(8,128)(2,1)} fusion(bf16[4,8,2,32,512]{4,3,2,1,0:T(8,128)(2,1)} %bitcast.60, s32[]{:T(128)S(6)} %select_n.70), kind=kLoop, calls=%fused_computation.9 | loop fusion | bytes 2097156 | tf_op jit(solution)/shard_map/jit(dynamic_index_in_dim)/squeeze | solution.py:165
  91.5 1.7 %fusion = bf16[4,8,32,512]{3,2,1,0:T(8,128)(2,1)S(1)} fusion(bf16[4,8,32,512]{3,2,1,0:T(8,128)(2,1)} %collective-permute-done.4, bf16[4,8,2,32,512]{4,3,2,1,0:T(8,128)(2,1)S(1)} %bitcast.59, s32[]{:T(128)S(6)} %select_n.69), kind=kLoop, calls=%fused_computation.1 | loop fusion | flops 2097152 | bytes 3145732 | tf_op jit(solution)/shard_map/convert_element_type | solution.py:169
  93.3 0.8 dynamic-slice_bitcast_fusion.2
  94.1 0.8 collective-permute-start.5
  94.9 1.6 %fusion.1 = bf16[4,8,32,512]{3,2,1,0:T(8,128)(2,1)S(1)} fusion(bf16[4,8,32,512]{3,2,1,0:T(8,128)(2,1)} %collective-permute-done, bf16[4,8,2,32,512]{4,3,2,1,0:T(8,128)(2,1)S(1)} %bitcast.61, s32[]{:T(128)S(6)} %select_n.69), kind=kLoop, calls=%fused_computation.3 | loop fusion | flops 2097152 | bytes 3145732 | tf_op jit(solution)/shard_map/convert_element_type | solution.py:169
  96.5 0.8 dynamic-slice_bitcast_fusion.3
  97.4 1.2 collective-permute-start.1
  98.6 10.5 %collective-permute-done.5 = bf16[4,4,32,512]{3,2,1,0:T(8,128)(2,1)S(1)} collective-permute-done((bf16[4,4,32,512]{3,2,1,0:T(8,128)(2,1)}, bf16[4,4,32,512]{3,2,1,0:T(8,128)(2,1)S(1)}, u32[]{:S(2)}, u32[]{:S(2)}) %collective-permute-start.5) | collective-permute-done | bytes 524320 | tf_op jit(solution)/shard_map/ppermute | solution.py:166
  109.3 1.3 collective-permute-start.6
  110.5 9.3 %collective-permute-done.1 = bf16[4,4,32,512]{3,2,1,0:T(8,128)(2,1)S(1)} collective-permute-done((bf16[4,4,32,512]{3,2,1,0:T(8,128)(2,1)}, bf16[4,4,32,512]{3,2,1,0:T(8,128)(2,1)S(1)}, u32[]{:S(2)}, u32[]{:S(2)}) %collective-permute-start.1) | collective-permute-done | bytes 524320 | tf_op jit(solution)/shard_map/ppermute | solution.py:166
  120.0 0.8 collective-permute-start.2
  120.9 1.1 collective-permute-start.7
  122.0 8.7 %collective-permute-done.2 = bf16[4,2,32,512]{3,2,1,0:T(8,128)(2,1)S(1)} collective-permute-done((bf16[4,2,32,512]{3,2,1,0:T(8,128)(2,1)S(1)}, bf16[4,2,32,512]{3,2,1,0:T(8,128)(2,1)S(1)}, u32[]{:S(2)}, u32[]{:S(2)}) %collective-permute-start.2) | collective-permute-done | bytes 262176 | tf_op jit(solution)/shard_map/ppermute | solution.py:166
  131.9 6.0 %collective-permute-done.3 = bf16[4,1,32,512]{3,2,1,0:T(8,128)(2,1)S(1)} collective-permute-done((bf16[4,1,32,512]{3,2,1,0:T(8,128)(2,1)S(1)}, bf16[4,1,32,512]{3,2,1,0:T(8,128)(2,1)S(1)}, u32[]{:S(2)}, u32[]{:S(2)}) %collective-permute-start.3) | collective-permute-done | bytes 131104 | tf_op jit(solution)/shard_map/ppermute | solution.py:166
  (33 shorter events, 8.6 us)
Async XLA Ops:
  29.7 15.7 %all-to-all-start.1 = ((bf16[16,24,512]{2,1,0:T(8,128)(2,1)}), bf16[16,24,512]{2,1,0:T(8,128)(2,1)S(1)}, u32[]{:S(2)}, u32[]{:S(2)}) async-start(bf16[16,24,512]{2,1,0:T(8,128)(2,1)} %bitcast.3), calls=%async_computation.1 | async-start | bytes 786432 | tf_op jit(solution)/shard_map/all_to_all | solution.py:197
  45.4 0.7 copy-start.3
  60.2 15.7 %all-to-all-start.2 = ((bf16[16,24,512]{2,1,0:T(8,128)(2,1)}), bf16[16,24,512]{2,1,0:T(8,128)(2,1)S(1)}, u32[]{:S(2)}, u32[]{:S(2)}) async-start(bf16[16,24,512]{2,1,0:T(8,128)(2,1)} %bitcast.71), calls=%async_computation.2 | async-start | bytes 786432 | tf_op jit(solution)/shard_map/all_to_all | solution.py:197
  66.3 25.2 %collective-permute-start.4 = (bf16[4,8,32,512]{3,2,1,0:T(8,128)(2,1)}, bf16[4,8,32,512]{3,2,1,0:T(8,128)(2,1)}, u32[]{:S(2)}, u32[]{:S(2)}) collective-permute-start(bf16[4,8,32,512]{3,2,1,0:T(8,128)(2,1)} %dynamic-slice_bitcast_fusion), channel_id=1, source_target_pairs={{0,1},{1,0},{2,3},{3,2},{4,5},{5,4},{6,7},{7,6},{8,9},{9,8},{10,11... | collective-permute-start | bytes 3145736 | tf_op jit(solution)/shard_map/ppermute | solution.py:166
  75.9 0.8 copy-start.2
  88.9 2.7 %copy-start = (bf16[4,512,512]{2,1,0:T(8,128)(2,1)S(1)}, bf16[4,512,512]{2,1,0:T(8,128)(2,1)}, u32[]{:S(2)}) copy-start(bf16[4,512,512]{2,1,0:T(8,128)(2,1)} %get-tuple-element.20) | copy-start | bytes 6291460
  91.4 3.5 %collective-permute-start = (bf16[4,8,32,512]{3,2,1,0:T(8,128)(2,1)}, bf16[4,8,32,512]{3,2,1,0:T(8,128)(2,1)}, u32[]{:S(2)}, u32[]{:S(2)}) collective-permute-start(bf16[4,8,32,512]{3,2,1,0:T(8,128)(2,1)} %dynamic-slice_bitcast_fusion.1), channel_id=1, source_target_pairs={{0,1},{1,0},{2,3},{3,2},{4,5},{5,4},{6,7},{7,6},{8,9},{9,8},{10,11... | collective-permute-start | bytes 3145736 | tf_op jit(solution)/shard_map/ppermute | solution.py:166
  91.5 3.4 %copy-start.1 = (bf16[4,512,512]{2,1,0:T(8,128)(2,1)S(1)}, bf16[4,512,512]{2,1,0:T(8,128)(2,1)}, u32[]{:S(2)}) copy-start(bf16[4,512,512]{2,1,0:T(8,128)(2,1)} %get-tuple-element.19) | copy-start | bytes 6291460
  94.1 14.9 %collective-permute-start.5 = (bf16[4,4,32,512]{3,2,1,0:T(8,128)(2,1)}, bf16[4,4,32,512]{3,2,1,0:T(8,128)(2,1)S(1)}, u32[]{:S(2)}, u32[]{:S(2)}) collective-permute-start(bf16[4,4,32,512]{3,2,1,0:T(8,128)(2,1)} %dynamic-slice_bitcast_fusion.2), channel_id=1, source_target_pairs={{0,2},{1,3},{2,0},{3,1},{4,6},{5,7},{6,4},{7,5},{8,10},{9,11},{10,... | collective-permute-start | bytes 1572872 | tf_op jit(solution)/shard_map/ppermute | solution.py:166
  97.4 22.4 %collective-permute-start.1 = (bf16[4,4,32,512]{3,2,1,0:T(8,128)(2,1)}, bf16[4,4,32,512]{3,2,1,0:T(8,128)(2,1)S(1)}, u32[]{:S(2)}, u32[]{:S(2)}) collective-permute-start(bf16[4,4,32,512]{3,2,1,0:T(8,128)(2,1)} %dynamic-slice_bitcast_fusion.3), channel_id=1, source_target_pairs={{0,2},{1,3},{2,0},{3,1},{4,6},{5,7},{6,4},{7,5},{8,10},{9,11},{10,... | collective-permute-start | bytes 1572872 | tf_op jit(solution)/shard_map/ppermute | solution.py:166
  109.3 11.6 %collective-permute-start.6 = (bf16[4,2,32,512]{3,2,1,0:T(8,128)(2,1)S(1)}, bf16[4,2,32,512]{3,2,1,0:T(8,128)(2,1)S(1)}, u32[]{:S(2)}, u32[]{:S(2)}) collective-permute-start(bf16[4,2,32,512]{3,2,1,0:T(8,128)(2,1)S(1)} %dynamic-slice_bitcast_fusion.4), channel_id=1, source_target_pairs={{0,4},{1,5},{2,6},{3,7},{4,0},{5,1},{6,2},{7,3},{8,12},{9,13},{10,... | collective-permute-start | bytes 786440 | tf_op jit(solution)/shard_map/ppermute | solution.py:166
  120.0 10.7 %collective-permute-start.2 = (bf16[4,2,32,512]{3,2,1,0:T(8,128)(2,1)S(1)}, bf16[4,2,32,512]{3,2,1,0:T(8,128)(2,1)S(1)}, u32[]{:S(2)}, u32[]{:S(2)}) collective-permute-start(bf16[4,2,32,512]{3,2,1,0:T(8,128)(2,1)S(1)} %dynamic-slice_bitcast_fusion.5), channel_id=1, source_target_pairs={{0,4},{1,5},{2,6},{3,7},{4,0},{5,1},{6,2},{7,3},{8,12},{9,13},{10,... | collective-permute-start | bytes 786440 | tf_op jit(solution)/shard_map/ppermute | solution.py:166
  120.9 10.2 %collective-permute-start.7 = (bf16[4,1,32,512]{3,2,1,0:T(8,128)(2,1)S(1)}, bf16[4,1,32,512]{3,2,1,0:T(8,128)(2,1)S(1)}, u32[]{:S(2)}, u32[]{:S(2)}) collective-permute-start(bf16[4,1,32,512]{3,2,1,0:T(8,128)(2,1)S(1)} %constant_dynamic-slice_fusion), channel_id=1, source_target_pairs={{0,8},{1,9},{2,10},{3,11},{4,12},{5,13},{6,14},{7,15},{8,0},{9,1},... | collective-permute-start | bytes 393224 | tf_op jit(solution)/shard_map/ppermute | solution.py:166
  130.9 7.1 %collective-permute-start.3 = (bf16[4,1,32,512]{3,2,1,0:T(8,128)(2,1)S(1)}, bf16[4,1,32,512]{3,2,1,0:T(8,128)(2,1)S(1)}, u32[]{:S(2)}, u32[]{:S(2)}) collective-permute-start(bf16[4,1,32,512]{3,2,1,0:T(8,128)(2,1)S(1)} %constant_dynamic-slice_fusion.1), channel_id=1, source_target_pairs={{0,8},{1,9},{2,10},{3,11},{4,12},{5,13},{6,14},{7,15},{8,0},{9,1},... | collective-permute-start | bytes 393224 | tf_op jit(solution)/shard_map/ppermute | solution.py:166

commit v2 on v1

v2 whole, which is shorter than its diff:
```python
import functools

import jax
import jax.numpy as jnp
from jax import lax
from jax.experimental import pallas as pl
from jax.experimental.pallas import tpu as pltpu
from jax.sharding import PartitionSpec as P

HEADS = 8
LANES = 128
NEG = -1e30
FAR = 1e9
VMEM_LIMIT = 56 * 1024 * 1024
f32, bf16 = jnp.float32, jnp.bfloat16


def dot_nn(a, b):
    return lax.dot_general(a, b, (((1,), (0,)), ((), ())), preferred_element_type=f32)


def dot_nt(a, b):
    return lax.dot_general(a, b, (((1,), (1,)), ((), ())), preferred_element_type=f32)


def dot_tn(a, b):
    return lax.dot_general(a, b, (((0,), (0,)), ((), ())), preferred_element_type=f32)


def project(x_ref, w_ref, q_ref, k_ref, v_ref):
    x = x_ref[...]
    q_ref[...] = (dot_nn(x, w_ref[0]) * 0.125).astype(bf16)
    k_ref[...] = dot_nn(x, w_ref[1]).astype(bf16)
    v_ref[...] = dot_nn(x, w_ref[2]).astype(bf16)


def probs_t(k2, qm, dist, width):
    s = jnp.where(dist <= width, dot_nt(k2, qm), NEG)
    e = jnp.exp(s - jnp.max(s, axis=0, keepdims=True))
    return e * (1.0 / jnp.sum(e, axis=0, keepdims=True))


def halves(pair):
    lane = lax.broadcasted_iota(jnp.int32, pair.shape, 1)
    low = lane < LANES // 2
    zero = jnp.zeros_like(pair)
    return jnp.where(low, pair, zero), jnp.where(low, zero, pair)


def merge(a, b):
    lane = lax.broadcasted_iota(jnp.int32, a.shape, 1)
    return jnp.where(lane < LANES // 2, a, b)


def forward_pairs(q_ref, k_ref, v_ref, dist_ref, m_ref, p_ref):
    @pl.loop(0, HEADS // 2)
    def _(pair):
        at = pl.ds(pl.multiple_of(pair * LANES, LANES), LANES)
        k2, v2 = k_ref[:, at], v_ref[:, at]
        outs = []
        for which, qm in enumerate(halves(q_ref[:, at])):
            p = probs_t(k2, qm, dist_ref[...], 0.5)
            p_ref[pair * 2 + which] = p
            outs.append(dot_tn(p.astype(bf16), v2))
        m_ref[:, at] = merge(*outs).astype(bf16)


def backward_pairs(q_ref, k_ref, v_ref, g_ref, probs_of, m_ref, dq_ref, dk_ref, dv_ref):
    @pl.loop(0, HEADS // 2)
    def _(pair):
        at = pl.ds(pl.multiple_of(pair * LANES, LANES), LANES)
        k2, v2 = k_ref[:, at], v_ref[:, at]
        q_parts, g_parts = halves(q_ref[:, at]), halves(g_ref[:, at])
        outs, dqs, dk, dv = [], [], 0.0, 0.0
        for which in range(2):
            qm, gm = q_parts[which], g_parts[which]
            p = probs_of(pair * 2 + which, k2, qm)
            pb = p.astype(bf16)
            if m_ref is not None:
                outs.append(dot_tn(pb, v2))
            dp = dot_nt(v2, gm).astype(bf16).astype(f32)
            ds = (p * (dp - jnp.sum(dp * p, axis=0, keepdims=True))).astype(bf16)
            dv = dv + dot_nn(pb, gm)
            dk = dk + dot_nn(ds, qm)
            dqs.append(dot_tn(ds, k2))
        if m_ref is not None:
            m_ref[:, at] = merge(*outs).astype(bf16)
        dq_ref[:, at] = (merge(*dqs) * 0.125).astype(bf16)
        dk_ref[:, at] = dk.astype(bf16)
        dv_ref[:, at] = dv.astype(bf16)


def back_sum(up, w_ref, dq_ref, dk_ref, dv_ref):
    back = up.astype(f32)
    for which, grad_ref in enumerate((dq_ref, dk_ref, dv_ref)):
        back = back + dot_nt(grad_ref[...], w_ref[which])
    return back


def reverse_bits(value, bits):
    return sum(((value >> b) & 1) << (bits - 1 - b) for b in range(bits))


def kernel(
    ranks, x_ref, cot_ref, cw_ref, rw_ref, start_ref, end_ref, windows_ref,
    grad_ref, col_out, row_out,
    q_ref, k_ref, v_ref, m_ref, rq_ref, rk_ref, rv_ref, rm_ref, og_ref, g_ref,
    dq_ref, dk_ref, dv_ref, up_ref, h_ref, wide_ref, dist_ref, p_ref,
    send_buf, cot_in, hid_in, back_buf, back_in,
    col_terms, row_terms, col_got, row_got,
    swap_send, swap_recv, sum_send, sum_recv,
):
    rows = x_ref.shape[0]
    block = rows // ranks
    bits = ranks.bit_length() - 1
    part = col_terms.shape[2]
    me = lax.axis_index("pos")

    barrier = pltpu.get_barrier_semaphore()

    @pl.loop(1, ranks)
    def _(step):
        pl.semaphore_signal(barrier, inc=1, device_id={"pos": lax.rem(me + step, ranks)})

    pl.semaphore_wait(barrier, ranks - 1)

    def swap_copy(which, src, dst, peer, slot):
        return pltpu.make_async_remote_copy(
            src_ref=src.at[peer],
            dst_ref=dst.at[slot],
            send_sem=swap_send.at[which, peer],
            recv_sem=swap_recv.at[which, slot],
            device_id={"pos": peer},
        )

    def swap_start(which, src, dst):
        @pl.loop(0, ranks - 1)
        def _(step):
            shift = 1 + lax.rem(step + ranks // 2 - 1, ranks - 1)
            swap_copy(which, src, dst, lax.rem(me + shift, ranks), me).start()

        dst[me] = src[me]

    def swap_wait(which, src, dst):
        @pl.loop(1, ranks)
        def _(shift):
            peer = lax.rem(me + shift, ranks)
            swap_copy(which, src, dst, peer, peer).wait_recv()

    def swap_sent(which, src, dst):
        @pl.loop(1, ranks)
        def _(shift):
            swap_copy(which, src, dst, lax.rem(me + shift, ranks), me).wait_send()

    def scatter_blocks(value, dst):
        for r in range(ranks):
            dst[r] = value[r * block:(r + 1) * block].astype(bf16)

    def gather_blocks(src, dst):
        for r in range(ranks):
            wide_ref[r * block:(r + 1) * block, :] = src[r].astype(f32)
        dst[...] = wide_ref[...].astype(bf16)

    keeps, gives, begin = [], [], 0
    for b in range(bits):
        half = ranks >> (b + 1)
        mine = lax.rem(me // (1 << b), 2)
        gives.append(begin + (1 - mine) * half)
        begin = begin + mine * half
        keeps.append(begin)

    def sum_copy(which, terms, got, b, w):
        half = ranks >> (b + 1)
        mine = lax.rem(me // (1 << b), 2)
        return pltpu.make_async_remote_copy(
            src_ref=terms.at[w, pl.ds(gives[b], half)],
            dst_ref=got.at[w, pl.ds(ranks - 2 * half, half)],
            send_sem=sum_send.at[which, b, w],
            recv_sem=sum_recv.at[which, b, w],
            device_id={"pos": me + (1 - 2 * mine) * (1 << b)},
        )

    def put_term(terms, w, value):
        for r in range(ranks):
            terms[w, reverse_bits(r, bits)] = value[r * part:(r + 1) * part].astype(bf16)

    def sum_step(which, terms, got, out, b, w):
        half = ranks >> (b + 1)
        sum_copy(which, terms, got, b, w).wait_recv()
        held = pl.ds(keeps[b], half)
        total = terms[w, held].astype(f32) + got[w, ranks - 2 * half:ranks - half].astype(f32)
        if b == bits - 1:
            out[w] = total[0]
        else:
            terms[w, held] = total.astype(bf16)
            sum_copy(which, terms, got, b + 1, w).start()

    def row_steps(b):
        for w in (3, 0, 1, 2):
            sum_step(0, row_terms, row_got, row_out, b, w)

    swap_start(0, cot_ref, cot_in)
    at_j = lax.broadcasted_iota(jnp.int32, (rows, rows), 0)
    at_i = lax.broadcasted_iota(jnp.int32, (rows, rows), 1)
    starts, ends = start_ref[...], end_ref[...]
    covers = ((me >= starts) & (me < ends)).astype(f32)
    cov = jnp.sum(jnp.where(at_j == at_i, covers, 0.0), axis=1, keepdims=True)
    dist_ref[...] = jnp.where((cov > 0.5) | (at_i == at_j), 0.0, FAR)
    project(x_ref, cw_ref, q_ref, k_ref, v_ref)
    forward_pairs(q_ref, k_ref, v_ref, dist_ref, m_ref, p_ref)
    wide_ref[...] = x_ref[...].astype(f32) + dot_nn(m_ref[...], cw_ref[3]) * cov
    scatter_blocks(wide_ref[...], send_buf)
    swap_start(1, send_buf, hid_in)

    sub = lax.broadcasted_iota(jnp.int32, (rows, 1), 0).astype(f32)
    lane = lax.broadcasted_iota(jnp.int32, (1, rows), 1).astype(f32)
    place_j, place_i = jnp.floor((sub + 0.5) / block), jnp.floor((lane + 0.5) / block)
    read_j, read_i = sub - block * place_j, lane - block * place_i
    own = lane == me.astype(f32) * block + read_j
    start_j = jnp.sum(jnp.where(own, starts.astype(f32), 0.0), axis=1, keepdims=True)
    end_j = jnp.sum(jnp.where(own, ends.astype(f32), 0.0), axis=1, keepdims=True)
    row_cov = ((place_j >= start_j) & (place_j < end_j)).astype(f32)
    gap = jnp.abs(place_j - place_i)
    dist_ref[...] = jnp.where((read_j == read_i) & ((row_cov > 0.5) | (gap == 0.0)), gap, FAR)
    swap_wait(0, cot_ref, cot_in)
    gather_blocks(cot_in, up_ref)
    og_ref[...] = (up_ref[...].astype(f32) * row_cov).astype(bf16)
    g_ref[...] = dot_nt(og_ref[...], rw_ref[3]).astype(bf16)
    swap_wait(1, send_buf, hid_in)
    gather_blocks(hid_in, h_ref)
    project(h_ref, rw_ref, rq_ref, rk_ref, rv_ref)
    backward_pairs(
        rq_ref, rk_ref, rv_ref, g_ref,
        lambda head, k2, qm: probs_t(k2, qm, dist_ref[...], windows_ref[head].astype(f32)),
        rm_ref, dq_ref, dk_ref, dv_ref,
    )
    wide_ref[...] = back_sum(up_ref[...], rw_ref, dq_ref, dk_ref, dv_ref)
    scatter_blocks(wide_ref[...], back_buf)
    swap_start(2, back_buf, back_in)
    for w, left, right in (
        (3, rm_ref, og_ref), (0, h_ref, dq_ref), (1, h_ref, dk_ref), (2, h_ref, dv_ref)
    ):
        put_term(row_terms, w, dot_tn(left[...], right[...]))
        sum_copy(0, row_terms, row_got, 0, w).start()
    row_steps(0)

    swap_wait(2, back_buf, back_in)
    gather_blocks(back_in, up_ref)
    og_ref[...] = (up_ref[...].astype(f32) * cov).astype(bf16)
    put_term(col_terms, 3, dot_tn(m_ref[...], og_ref[...]))
    sum_copy(1, col_terms, col_got, 0, 3).start()
    g_ref[...] = dot_nt(og_ref[...], cw_ref[3]).astype(bf16)
    row_steps(1)
    backward_pairs(
        q_ref, k_ref, v_ref, g_ref, lambda head, k2, qm: p_ref[head], None, dq_ref, dk_ref, dv_ref
    )
    sum_step(1, col_terms, col_got, col_out, 0, 3)
    for w, right in enumerate((dq_ref, dk_ref, dv_ref)):
        put_term(col_terms, w, dot_tn(x_ref[...], right[...]))
        sum_copy(1, col_terms, col_got, 0, w).start()
        if w > 0:
            sum_step(1, col_terms, col_got, col_out, 0, w - 1)
    sum_step(1, col_terms, col_got, col_out, 0, 2)
    for b in range(2, bits):
        row_steps(b)
    grad_ref[...] = back_sum(up_ref[...], cw_ref, dq_ref, dk_ref, dv_ref).astype(bf16)
    for b in range(1, bits):
        for w in (3, 0, 1, 2):
            sum_step(1, col_terms, col_got, col_out, b, w)

    swap_sent(0, cot_ref, cot_in)
    swap_sent(1, send_buf, hid_in)
    swap_sent(2, back_buf, back_in)
    for b in range(bits):
        for w in range(4):
            sum_copy(0, row_terms, row_got, b, w).wait_send()
            sum_copy(1, col_terms, col_got, b, w).wait_send()


def shards(inputs, cotangent, col_weights, row_weights, read_start, read_end, windows):
    rows, local_pos, width = inputs.shape
    ranks = lax.axis_size("pos")
    block, part, bits = rows // ranks, width // ranks, ranks.bit_length() - 1
    act = pltpu.VMEM((rows, width), bf16)
    blocks = pltpu.VMEM((ranks, block, width), bf16)
    terms = pltpu.VMEM((4, ranks, part, width), bf16)
    sums = jax.ShapeDtypeStruct((4, part, width), f32)
    spec = pl.BlockSpec(memory_space=pltpu.VMEM)
    grad, col_sums, row_sums = pl.pallas_call(
        functools.partial(kernel, ranks),
        out_shape=[jax.ShapeDtypeStruct((rows, width), bf16), sums, sums],
        in_specs=[spec] * 6 + [pl.BlockSpec(memory_space=pltpu.SMEM)],
        out_specs=[spec] * 3,
        scratch_shapes=[act] * 15
        + [pltpu.VMEM((rows, width), f32), pltpu.VMEM((rows, rows), f32)]
        + [pltpu.VMEM((HEADS, rows, rows), f32)]
        + [blocks] * 5
        + [terms] * 4
        + [pltpu.SemaphoreType.DMA((3, ranks))] * 2
        + [pltpu.SemaphoreType.DMA((2, bits, 4))] * 2,
        compiler_params=pltpu.CompilerParams(
            vmem_limit_bytes=VMEM_LIMIT, collective_id=0, has_side_effects=True
        ),
    )(
        inputs.reshape(rows, width),
        cotangent.reshape(ranks, block, width),
        col_weights,
        row_weights,
        read_start.reshape(1, rows),
        read_end.reshape(1, rows),
        windows,
    )
    return (grad.reshape(inputs.shape), col_sums, row_sums)


def solution(mesh):
    return jax.shard_map(
        shards,
        mesh=mesh,
        in_specs=(P("grp", "pos", None), P("grp", "pos", None), P(), P(), P("grp"), P("grp"), P()),
        out_specs=(P("grp", "pos", None), P("grp", "pos", None), P("grp", "pos", None)),
        check_vma=False,
    )
```

time: 139 us -> 94.3 us (0.68)
  waiting for transfers between devices: 52.3 us -> 0 us
  Pallas kernels: 34.1 us -> 85.8 us
  blocking collectives: 19.7 us -> 0 us
  starting transfers between devices: 13.1 us -> 0 us
  other arithmetic: 6.61 us -> 0 us
  local copies, waits for them, and re-layouts: 12.1 us -> 7.6 us
    pallas_call x3 -> x1, Pallas kernels: 34.1 us -> 85.8 us  [shards(): pl.pallas_call(functools.partial(kernel, ranks), out_shape=[jax.ShapeDtyp...]
    ppermute x8 -> x0, waiting for transfers between devices: 34.5 us -> none  [reduce_rows(): got = lax.ppermute(give, 'pos', [(r, r ^ 1 << bit) for r in range(ranks)])]
    all_to_all x1 -> x0, blocking collectives: 19.7 us -> none  [spread(): return swap(array.reshape(ranks, block, width)).reshape(rows, width)]
    all_to_all x2 -> x0, waiting for transfers between devices: 17.9 us -> none  [spread(): return swap(array.reshape(ranks, block, width)).reshape(rows, width)]
    all_to_all x2 -> x0, starting transfers between devices: 7.29 us -> none  [spread(): return swap(array.reshape(ranks, block, width)).reshape(rows, width)]
    squeeze x8 -> x0, local copies, waits for them, and re-layouts: 6.66 us -> none  [reduce_rows(): give = lax.dynamic_index_in_dim(split, 1 - mine, 2, keepdims=False)]
    ppermute x8 -> x0, starting transfers between devices: 5.82 us -> none  [reduce_rows(): got = lax.ppermute(give, 'pos', [(r, r ^ 1 << bit) for r in range(ranks)])]
    convert_element_type x8 -> x0, other arithmetic: 4.41 us -> none  [the longest x6 3.8 us: reduce_rows(): held = total if 1 << bit >= ranks else total.astype(bf16)]
  transfers between devices with their start and end apart: 10 -> 0, of which waited for: 6 -> 0; matrix products, arithmetic and copies ran while one was open for 11% -> 0% of each run, Pallas kernels for 9% -> 0%
where the time goes in v2:
time: 94.3 us; the launch traced here: 94 us
  Pallas kernels  85.8 us (91%)
  local copies, waits for them, and re-layouts  7.6 us (8%)
    pallas_call x1, Pallas kernels, shards(): pl.pallas_call(functools.partial(kernel, ranks), out_shape=[jax.ShapeDtyp...  85.8 us
    unnamed x3, local copies, waits for them, and re-layouts  5.11 us

profile of v2, /device:TPU:0, one launch (start us, length us, event | category | flops | bytes accessed | tf_op | source)
XLA Modules:
  0.0 94.0 jit_solution(10236425397156920969)
XLA Ops:
  0.6 1.2 %reshape.23.start_ref = s32[1,384]{1,0:T(1,128)} reshape(s32[384]{0:T(512)} %param.11) | data formatting | bytes 3072 | tf_op jit(solution)/shard_map/reshape | solution.py:309
  1.9 1.2 %reshape.24.end_ref = s32[1,384]{1,0:T(1,128)} reshape(s32[384]{0:T(512)} %param.12) | data formatting | bytes 3072 | tf_op jit(solution)/shard_map/reshape | solution.py:310
  3.1 85.8 %shard_map.94 = (bf16[384,512]{1,0:T(8,128)(2,1)}, f32[4,32,512]{2,1,0:T(8,128)}, f32[4,32,512]{2,1,0:T(8,128)}) custom-call(bf16[384,512]{1,0:T(8,128)(2,1)} %bitcast.4, bf16[16,24,512]{2,1,0:T(8,128)(2,1)} %bitcast.5, bf16[4,512,512]{2,1,0:T(8,128)(2,1)} %cw_ref.1, bf16[4,512,512]{2,1,0:T(8,128)(2,1)} %rw_ref.1, s32[1,384]{1,0:T(1,128)} %reshape.23.start_ref, ...), custom_call_target="tpu_custom_call" | custom-call | tf_op jit(solution)/shard_map/pallas_call | solution.py:289
  88.9 1.8 %copy.13 = bf16[384,1,512]{2,0,1:T(8,128)(2,1)} copy(bf16[384,1,512]{2,0,1:T(8,128)(2,1)} %bitcast.3) | data formatting | bytes 786432
  90.7 1.7 %copy.14 = f32[4,32,512]{2,1,0:T(8,128)} copy(f32[4,32,512]{2,1,0:T(8,128)} %get-tuple-element.13) | data formatting | bytes 524288
  92.4 1.7 %copy.15 = f32[4,32,512]{2,1,0:T(8,128)} copy(f32[4,32,512]{2,1,0:T(8,128)} %get-tuple-element.14) | data formatting | bytes 524288

commit v3 on v2

--- a/solution.py
+++ b/solution.py
@@ -11,6 +11,7 @@
 LANES = 128
 NEG = -1e30
 FAR = 1e9
+LATE_NEAR = (0,)
 VMEM_LIMIT = 56 * 1024 * 1024
 f32, bf16 = jnp.float32, jnp.bfloat16
 
@@ -97,10 +98,6 @@
     return back
 
 
-def reverse_bits(value, bits):
-    return sum(((value >> b) & 1) << (bits - 1 - b) for b in range(bits))
-
-
 def kernel(
     ranks, x_ref, cot_ref, cw_ref, rw_ref, start_ref, end_ref, windows_ref,
     grad_ref, col_out, row_out,
@@ -161,33 +158,42 @@
             wide_ref[r * block:(r + 1) * block, :] = src[r].astype(f32)
         dst[...] = wide_ref[...].astype(bf16)
 
-    keeps, gives, begin = [], [], 0
-    for b in range(bits):
-        half = ranks >> (b + 1)
-        mine = lax.rem(me // (1 << b), 2)
-        gives.append(begin + (1 - mine) * half)
-        begin = begin + mine * half
-        keeps.append(begin)
+    orders = [list(range(bits)) for _ in range(4)]
+    for w in LATE_NEAR:
+        orders[w] = [0] + list(range(2, bits)) + [1]
+    keeps, gives, partners = [], [], []
+    for w in range(4):
+        begin, keep, give, partner = 0, [], [], []
+        for b, bit in enumerate(orders[w]):
+            half = ranks >> (b + 1)
+            mine = lax.rem(me // (1 << bit), 2)
+            give.append(begin + (1 - mine) * half)
+            begin = begin + mine * half
+            keep.append(begin)
+            partner.append(me + (1 - 2 * mine) * (1 << bit))
+        keeps.append(keep)
+        gives.append(give)
+        partners.append(partner)
 
     def sum_copy(which, terms, got, b, w):
         half = ranks >> (b + 1)
-        mine = lax.rem(me // (1 << b), 2)
         return pltpu.make_async_remote_copy(
-            src_ref=terms.at[w, pl.ds(gives[b], half)],
+            src_ref=terms.at[w, pl.ds(gives[w][b], half)],
             dst_ref=got.at[w, pl.ds(ranks - 2 * half, half)],
             send_sem=sum_send.at[which, b, w],
             recv_sem=sum_recv.at[which, b, w],
-            device_id={"pos": me + (1 - 2 * mine) * (1 << b)},
+            device_id={"pos": partners[w][b]},
         )
 
     def put_term(terms, w, value):
         for r in range(ranks):
-            terms[w, reverse_bits(r, bits)] = value[r * part:(r + 1) * part].astype(bf16)
+            slot = sum(((r >> bit) & 1) << (bits - 1 - b) for b, bit in enumerate(orders[w]))
+            terms[w, slot] = value[r * part:(r + 1) * part].astype(bf16)
 
     def sum_step(which, terms, got, out, b, w):
         half = ranks >> (b + 1)
         sum_copy(which, terms, got, b, w).wait_recv()
-        held = pl.ds(keeps[b], half)
+        held = pl.ds(keeps[w][b], half)
         total = terms[w, held].astype(f32) + got[w, ranks - 2 * half:ranks - half].astype(f32)
         if b == bits - 1:
             out[w] = total[0]
@@ -242,18 +248,18 @@
     ):
         put_term(row_terms, w, dot_tn(left[...], right[...]))
         sum_copy(0, row_terms, row_got, 0, w).start()
-    row_steps(0)
 
     swap_wait(2, back_buf, back_in)
     gather_blocks(back_in, up_ref)
+    row_steps(0)
     og_ref[...] = (up_ref[...].astype(f32) * cov).astype(bf16)
     put_term(col_terms, 3, dot_tn(m_ref[...], og_ref[...]))
     sum_copy(1, col_terms, col_got, 0, 3).start()
     g_ref[...] = dot_nt(og_ref[...], cw_ref[3]).astype(bf16)
-    row_steps(1)
     backward_pairs(
         q_ref, k_ref, v_ref, g_ref, lambda head, k2, qm: p_ref[head], None, dq_ref, dk_ref, dv_ref
     )
+    row_steps(1)
     sum_step(1, col_terms, col_got, col_out, 0, 3)
     for w, right in enumerate((dq_ref, dk_ref, dv_ref)):
         put_term(col_terms, w, dot_tn(x_ref[...], right[...]))

time: 94.3 us -> 91.3 us (0.968)
  Pallas kernels: 85.8 us -> 82.8 us
    pallas_call x1, Pallas kernels: 85.8 us -> 82.8 us  [shards(): pl.pallas_call(functools.partial(kernel, ranks), out_shape=[jax.ShapeDtyp...]
where the time goes in v3:
time: 91.3 us; the launch traced here: 91 us
  Pallas kernels  82.8 us (91%)
  local copies, waits for them, and re-layouts  7.6 us (8%)
    pallas_call x1, Pallas kernels, shards(): pl.pallas_call(functools.partial(kernel, ranks), out_shape=[jax.ShapeDtyp...  82.8 us
    unnamed x3, local copies, waits for them, and re-layouts  5.11 us

profile of v3, /device:TPU:0, one launch (start us, length us, event | category | flops | bytes accessed | tf_op | source)
XLA Modules:
  0.0 91.0 jit_solution(6445365730219913571)
XLA Ops:
  0.6 1.2 %reshape.23.start_ref = s32[1,384]{1,0:T(1,128)} reshape(s32[384]{0:T(512)} %param.11) | data formatting | bytes 3072 | tf_op jit(solution)/shard_map/reshape | solution.py:315
  1.9 1.2 %reshape.24.end_ref = s32[1,384]{1,0:T(1,128)} reshape(s32[384]{0:T(512)} %param.12) | data formatting | bytes 3072 | tf_op jit(solution)/shard_map/reshape | solution.py:316
  3.1 82.8 %shard_map.94 = (bf16[384,512]{1,0:T(8,128)(2,1)}, f32[4,32,512]{2,1,0:T(8,128)}, f32[4,32,512]{2,1,0:T(8,128)}) custom-call(bf16[384,512]{1,0:T(8,128)(2,1)} %bitcast.4, bf16[16,24,512]{2,1,0:T(8,128)(2,1)} %bitcast.5, bf16[4,512,512]{2,1,0:T(8,128)(2,1)} %cw_ref.1, bf16[4,512,512]{2,1,0:T(8,128)(2,1)} %rw_ref.1, s32[1,384]{1,0:T(1,128)} %reshape.23.start_ref, ...), custom_call_target="tpu_custom_call" | custom-call | tf_op jit(solution)/shard_map/pallas_call | solution.py:295
  85.9 1.8 %copy.13 = bf16[384,1,512]{2,0,1:T(8,128)(2,1)} copy(bf16[384,1,512]{2,0,1:T(8,128)(2,1)} %bitcast.3) | data formatting | bytes 786432
  87.7 1.7 %copy.14 = f32[4,32,512]{2,1,0:T(8,128)} copy(f32[4,32,512]{2,1,0:T(8,128)} %get-tuple-element.13) | data formatting | bytes 524288
  89.4 1.7 %copy.15 = f32[4,32,512]{2,1,0:T(8,128)} copy(f32[4,32,512]{2,1,0:T(8,128)} %get-tuple-element.14) | data formatting | bytes 524288

commit v4 on v3

--- a/solution.py
+++ b/solution.py
@@ -133,7 +133,7 @@
     def swap_start(which, src, dst):
         @pl.loop(0, ranks - 1)
         def _(step):
-            shift = 1 + lax.rem(step + ranks // 2 - 1, ranks - 1)
+            shift = step + 1
             swap_copy(which, src, dst, lax.rem(me + shift, ranks), me).start()
 
         dst[me] = src[me]

time: 91.3 us -> 91.9 us (level)
  no operation moved by 1% of the time
where the time goes in v4:
time: 91.9 us; the launch traced here: 91.6 us
  Pallas kernels  83.4 us (91%)
  local copies, waits for them, and re-layouts  7.6 us (8%)
    pallas_call x1, Pallas kernels, shards(): pl.pallas_call(functools.partial(kernel, ranks), out_shape=[jax.ShapeDtyp...  83.4 us
    unnamed x3, local copies, waits for them, and re-layouts  5.11 us

profile of v4, /device:TPU:0, one launch (start us, length us, event | category | flops | bytes accessed | tf_op | source)
XLA Modules:
  0.0 91.6 jit_solution(12377377937570806825)
XLA Ops:
  0.6 1.2 %reshape.23.start_ref = s32[1,384]{1,0:T(1,128)} reshape(s32[384]{0:T(512)} %param.11) | data formatting | bytes 3072 | tf_op jit(solution)/shard_map/reshape | solution.py:315
  1.9 1.2 %reshape.24.end_ref = s32[1,384]{1,0:T(1,128)} reshape(s32[384]{0:T(512)} %param.12) | data formatting | bytes 3072 | tf_op jit(solution)/shard_map/reshape | solution.py:316
  3.1 83.4 %shard_map.94 = (bf16[384,512]{1,0:T(8,128)(2,1)}, f32[4,32,512]{2,1,0:T(8,128)}, f32[4,32,512]{2,1,0:T(8,128)}) custom-call(bf16[384,512]{1,0:T(8,128)(2,1)} %bitcast.4, bf16[16,24,512]{2,1,0:T(8,128)(2,1)} %bitcast.5, bf16[4,512,512]{2,1,0:T(8,128)(2,1)} %cw_ref.1, bf16[4,512,512]{2,1,0:T(8,128)(2,1)} %rw_ref.1, s32[1,384]{1,0:T(1,128)} %reshape.23.start_ref, ...), custom_call_target="tpu_custom_call" | custom-call | tf_op jit(solution)/shard_map/pallas_call | solution.py:295
  86.5 1.8 %copy.13 = bf16[384,1,512]{2,0,1:T(8,128)(2,1)} copy(bf16[384,1,512]{2,0,1:T(8,128)(2,1)} %bitcast.3) | data formatting | bytes 786432
  88.3 1.7 %copy.14 = f32[4,32,512]{2,1,0:T(8,128)} copy(f32[4,32,512]{2,1,0:T(8,128)} %get-tuple-element.13) | data formatting | bytes 524288
  90.0 1.7 %copy.15 = f32[4,32,512]{2,1,0:T(8,128)} copy(f32[4,32,512]{2,1,0:T(8,128)} %get-tuple-element.14) | data formatting | bytes 524288
